TPU v7x, 32 devices: a whole 2x2x4 slice. The times are simulated.
32 devices in a mesh: pool: 2 (over x), mp: 8 (over z, y), dp: 2 (over core).
Axes of the slice: x: 2, y: 2, z: 4, core: 2. Of those that a mesh axis runs over, the one named last changes fastest.
Arguments:
- tokens: bfloat16 [2048, 6144], P(('pool', 'dp'), 'mp'), parts along dimension 0, may hold values from -8 to 8
- ln_gain: float32 [6144], replicated, may hold values from 0.5 to 1.5
- qkv_weight: bfloat16 [6144, 3, 4096], P('dp', None, 'mp'), may hold values from -0.125 to 0.125
- q_gain: float32 [32, 128], P('mp'), may hold values from 0.5 to 9
- k_gain: float32 [32, 128], P('mp'), may hold values from 0.5 to 9
- out_weight: bfloat16 [4096, 6144], P('mp', 'dp'), may hold values from -0.125 to 0.125
- mlp_in: bfloat16 [6144, 12288], P('dp', 'mp'), may hold values from -0.078125 to 0.078125
- mlp_bias: float32 [12288], P('mp'), may hold values from -4 to 4
- mlp_out: bfloat16 [12288, 6144], P('mp', 'dp'), may hold values from -0.078125 to 0.078125
Outputs:
- mixed: bfloat16 [2048, 6144], P(('pool', 'dp'), 'mp'), parts along dimension 0
There are 2 independent parts, one for each index of `pool`. A program takes and returns all parts, laid end to end along the dimension named above; an argument that names none is the same for every part. Nothing has to cross between parts.
All inputs are finite; a program needn't handle non-finite values.
Results may differ from a plain program's by a relative error of at most 0.01.
Values may be sent and summed in bfloat16 or wider, within the bound.
A program may use at most 192 MiB of HBM per device.

v0:
```python
import math

import jax
import jax.numpy as jnp
from jax import lax
from jax.sharding import PartitionSpec as P

EPSILON = 1e-06


def normalize(values):
    centre = jnp.mean(values, axis=-1, keepdims=True)
    spread = jnp.mean(jnp.square(values - centre), axis=-1, keepdims=True)
    return (values - centre) * lax.rsqrt(spread + EPSILON)


def shards(tokens, ln_gain, qkv_weight, q_gain, k_gain, out_weight, mlp_in, mlp_bias, mlp_out):
    tok_rows = tokens.shape[0]
    gathered = lax.all_gather(tokens, "mp", axis=1, tiled=True)
    normed = (normalize(gathered.astype(jnp.float32)) * ln_gain).astype(jnp.bfloat16)
    rows_part = qkv_weight.shape[0]
    qkv_local = qkv_weight.reshape(rows_part, -1)
    pieces = (
        lax.all_gather(qkv_local, "dp", axis=0, tiled=True),
        lax.all_gather(mlp_in, "dp", axis=0, tiled=True),
    )
    projected = jnp.dot(normed, pieces[0], preferred_element_type=jnp.float32)
    pre_act = jnp.dot(normed, pieces[1], preferred_element_type=jnp.float32)
    head_count = q_gain.shape[0]
    head_size = q_gain.shape[1]
    projected = projected.reshape(tok_rows, 3, head_count, head_size)
    queries = (normalize(projected[:, 0]) * q_gain).astype(jnp.bfloat16)
    key_rows = (normalize(projected[:, 1]) * k_gain).astype(jnp.bfloat16)
    value_rows = projected[:, 2].astype(jnp.bfloat16)
    clip_keys, clip_values = (
        lax.all_gather(key_rows, "dp", axis=0, tiled=True),
        lax.all_gather(value_rows, "dp", axis=0, tiled=True),
    )
    scores = jnp.einsum("qhd,khd->hqk", queries, clip_keys, preferred_element_type=jnp.float32) * (
        1.0 / math.sqrt(head_size)
    )
    probs = jax.nn.softmax(scores, axis=-1).astype(jnp.bfloat16)
    attended = jnp.einsum("hqk,khd->qhd", probs, clip_values, preferred_element_type=jnp.float32)
    attended = attended.astype(jnp.bfloat16).reshape(tok_rows, head_count * head_size)
    hidden = jax.nn.gelu(pre_act + mlp_bias, approximate=False).astype(jnp.bfloat16)
    pieces = lax.all_gather((out_weight, mlp_out), "dp", axis=1, tiled=True)
    result = jnp.dot(attended, pieces[0], preferred_element_type=jnp.float32)
    branch_terms = result + jnp.dot(hidden, pieces[1], preferred_element_type=jnp.float32)
    summed = lax.psum_scatter(
        branch_terms.astype(jnp.bfloat16), "mp", scatter_dimension=1, tiled=True
    ).astype(jnp.float32)
    return (tokens.astype(jnp.float32) + summed).astype(jnp.bfloat16)


def solution(mesh):
    return jax.shard_map(
        shards,
        mesh=mesh,
        in_specs=(
            P(("pool", "dp"), "mp"),
            P(),
            P("dp", None, "mp"),
            P("mp", None),
            P("mp", None),
            P("mp", "dp"),
            P("dp", "mp"),
            P("mp"),
            P("mp", "dp"),
        ),
        out_specs=P(("pool", "dp"), "mp"),
        check_vma=False,
    )
```

profile of v0, /device:TPU:8, one launch (start us, length us, event | category | flops | bytes accessed | tf_op | source)
XLA Modules:
  0.0 406.5 jit_solution(6420252062567651065)
XLA Ops:
  7.3 12.7 %copy.13 = bf16[3072,3,512]{0,2,1:T(8,128)(2,1)} copy(bf16[3072,3,512]{2,0,1:T(8,128)(2,1)} %param.11) | data formatting | bytes 18874368 | tf_op args[2]
  20.8 88.4 %all-gather.9.cloned.1.call-done = bf16[512,6144]{1,0:T(8,128)(2,1)} async-done(((bf16[512,768]{1,0:T(8,128)(2,1)}), bf16[512,6144]{1,0:T(8,128)(2,1)}) %all-gather.9.cloned.1.call-update) | async-done | bytes 6291472 | tf_op jit(solution)/shard_map/all_gather | solution.py:19
  109.2 3.8 convert_reduce_fusion
  113.0 0.7 copy-done
  113.8 1.8 fusion.3
  115.5 28.2 %all-gather.11.cloned.1.call-done = bf16[6144,1536]{0,1:T(8,128)(2,1)} async-done(((bf16[3072,1536]{0,1:T(8,128)(2,1)}), bf16[6144,1536]{0,1:T(8,128)(2,1)}) %all-gather.11.cloned.1.call-update) | async-done | bytes 18874384 | tf_op jit(solution)/shard_map/all_gather | solution.py:24
  143.7 17.6 %fusion.30 = f32[512,1536]{1,0:T(8,128)} fusion(bf16[6144,1536]{0,1:T(8,128)(2,1)} %all-gather.11.cloned.1.call-done, bf16[512,6144]{1,0:T(8,128)(2,1)} %all-gather.9.cloned.1.call-done, f32[6144]{0:T(1024)S(1)} %copy-done.4, f32[512]{0:T(512)S(1)} %add_rsqrt_fusion.2, f32[512]{0:T(512)S(1)} %broadcast_multiply_fusion.2), kind=kOutput, calls=%fused_computation.57 | convolution fusion | flops 9679405056 | bytes 28340224 | tf_op jit(solution)/shard_map/dot_general | solution.py:27
  161.3 3.7 reshape.53
  165.0 3.1 slice_reduce_fusion.1
  168.1 1.1 copy.20
  169.3 2.2 multiply_reduce_fusion.1
  171.5 2.4 multiply_convert_fusion
  174.0 1.0 slice.13
  175.0 2.1 copy.21
  179.6 0.8 all-gather.17.cloned.1.call-done
  180.3 22.4 %fusion.13 = bf16[512,1536]{1,0:T(8,128)(2,1)S(1)} fusion(bf16[6144,1536]{1,0:T(8,128)(2,1)} %all-gather.17.cloned.1.call-done, f32[1536]{0:T(1024)S(1)} %copy-done.5, bf16[512,6144]{1,0:T(8,128)(2,1)} %all-gather.9.cloned.1.call-done, f32[6144]{0:T(1024)S(1)} %copy-done.4, f32[512]{0:T(512)S(1)} %add_rsqrt_fusion.2, f32[512]{0:T(512)S(1)} %broadcast_multiply_fusion.2), kind=kOutput, calls=%fused_computation.19 | convolution fusion | flops 9731309568 | bytes 26773504 | tf_op jit(solution)/shard_map/dot_general | solution.py:28
  202.8 7.3 %fusion.32 = (f32[4,512]{1,0:T(4,128)S(1)}, f32[4,512,1024]{2,1,0:T(8,128)}) fusion(bf16[1024,4,128]{2,0,1:T(8,128)(2,1)} %all-gather.13.cloned.1.call-done, f32[512,1,4,128]{3,2,1,0:T(4,128)S(1)} %copy-done.1, f32[4,128]{1,0:T(4,128)S(1)} %copy-done.6, f32[512,4]{0,1:T(4,128)S(1)} %add_rsqrt_fusion.1, f32[512,4]{0,1:T(4,128)S(1)} %broadcast_multiply_fusion.1), kind=kOutput, calls=%fused_computation.58 | convolution fusion | flops 544211968 | bytes 10512384 | tf_op jit(solution)/shard_map/sub | solution.py:42
  210.1 6.1 %fusion.21 = bf16[4,128,512]{2,1,0:T(8,128)(2,1)S(1)} fusion(f32[4,512,1024]{2,1,0:T(8,128)} %get-tuple-element.10, f32[4,512]{1,0:T(4,128)S(1)} %get-tuple-element.9, bf16[1024,1,4,128]{0,3,2,1:T(8,128)(2,1)} %all-gather.21.cloned.1.call-done), kind=kOutput, calls=%fused_computation.36 | convolution fusion | flops 541327360 | bytes 9969664 | tf_op jit(solution)/shard_map/hqk,khd->qhd/dot_general | solution.py:43
  216.2 6.7 %all-gather.15.cloned.1.call-done = bf16[512,6144]{1,0:T(8,128)(2,1)} async-done(((bf16[512,3072]{1,0:T(8,128)(2,1)}), bf16[512,6144]{1,0:T(8,128)(2,1)}) %all-gather.15.cloned.1.call-update) | async-done | bytes 6291472 | tf_op jit(solution)/shard_map/all_gather | solution.py:46
  223.0 9.3 %fusion.33 = f32[512,6144]{1,0:T(8,128)} fusion(bf16[512,512]{0,1:T(8,128)(2,1)S(1)} %bitcast.42, bf16[512,6144]{1,0:T(8,128)(2,1)} %all-gather.15.cloned.1.call-done), kind=kOutput, calls=%fused_computation.59 | convolution fusion | flops 3221225472 | bytes 19398656 | tf_op jit(solution)/shard_map/dot_general | solution.py:47
  232.3 27.2 %all-gather.19.cloned.1.call-done = bf16[1536,6144]{1,0:T(8,128)(2,1)} async-done(((bf16[1536,3072]{1,0:T(8,128)(2,1)}), bf16[1536,6144]{1,0:T(8,128)(2,1)}) %all-gather.19.cloned.1.call-update) | async-done | bytes 18874384 | tf_op jit(solution)/shard_map/all_gather | solution.py:46
  259.5 19.6 %add_convert_fusion = bf16[512,6144]{1,0:T(8,128)(2,1)} fusion(f32[512,6144]{1,0:T(8,128)} %fusion.33, bf16[512,1536]{1,0:T(8,128)(2,1)S(1)} %fusion.13, bf16[1536,6144]{1,0:T(8,128)(2,1)} %all-gather.19.cloned.1.call-done), kind=kOutput, calls=%fused_computation.8 | convolution fusion | flops 9669967872 | bytes 39321600 | tf_op jit(solution)/shard_map/dot_general | solution.py:48
  279.2 118.3 %reduce-scatter.2.cloned.1.call-done = bf16[512,768]{1,0:T(8,128)(2,1)} async-done(((bf16[512,6144]{1,0:T(8,128)(2,1)}), bf16[512,768]{1,0:T(8,128)(2,1)}) %reduce-scatter.2.cloned.1.call-update) | async-done | bytes 786448 | tf_op jit(solution)/shard_map/reduce_scatter | solution.py:49
  397.4 2.2 add_convert_fusion.1
  (39 shorter events, 4.1 us)
Async XLA Ops:
  6.5 102.6 %all-gather.9.cloned.1.call-start = ((), (), s32[]{:S(2)}) async-start(), calls=%async_computation.1 | async-start | bytes 7077888 | tf_op jit(solution)/shard_map/all_gather | solution.py:19
  7.3 136.5 %all-gather.11.cloned.1.call-start = ((), (), s32[]{:S(2)}) async-start(), calls=%async_computation.2 | async-start | bytes 28311552 | tf_op jit(solution)/shard_map/all_gather | solution.py:24
  20.0 160.3 %all-gather.17.cloned.1.call-start = ((), (), s32[]{:S(2)}) async-start(), calls=%async_computation.5 | async-start | bytes 28311552 | tf_op jit(solution)/shard_map/all_gather | solution.py:25
  20.7 182.1 %all-gather.13.cloned.1.call-start = ((), (), s32[]{:S(2)}) async-start(), calls=%async_computation.3 | async-start | bytes 1572864 | tf_op jit(solution)/shard_map/all_gather | solution.py:36
  109.2 4.6 %copy-start = (bf16[512,6144]{1,0:T(8,128)(2,1)S(1)}, bf16[512,6144]{1,0:T(8,128)(2,1)}, u32[]{:S(2)}) copy-start(bf16[512,6144]{1,0:T(8,128)(2,1)} %all-gather.9.cloned.1.call-done) | copy-start | bytes 18874372
  113.8 30.0 %copy-start.4 = (f32[6144]{0:T(1024)S(1)}, f32[6144]{0:T(1024)}, u32[]{:S(2)}) copy-start(f32[6144]{0:T(1024)} %param.10) | copy-start | bytes 73732
  165.0 6.5 %copy-start.3 = (f32[4,128]{1,0:T(4,128)S(1)}, f32[4,128]{1,0:T(4,128)}, u32[]{:S(2)}) copy-start(f32[4,128]{1,0:T(4,128)} %param.13) | copy-start | bytes 6148
  173.9 36.1 %all-gather.21.cloned.1.call-start = ((), (), s32[]{:S(2)}) async-start(), calls=%async_computation.8 | async-start | bytes 1572864 | tf_op jit(solution)/shard_map/all_gather | solution.py:37
  177.1 45.9 %all-gather.15.cloned.1.call-start = ((), (), s32[]{:S(2)}) async-start(), calls=%async_computation.4 | async-start | bytes 9437184 | tf_op jit(solution)/shard_map/all_gather | solution.py:46
  177.7 1.2 copy-start.1
  177.7 2.6 copy-start.5
  177.7 81.8 %all-gather.19.cloned.1.call-start = ((), (), s32[]{:S(2)}) async-start(), calls=%async_computation.6 | async-start | bytes 28311552 | tf_op jit(solution)/shard_map/all_gather | solution.py:46
  178.4 219.0 %reduce-scatter.2.cloned.1.call-start = ((), (), s32[]{:S(2)}) async-start(), calls=%async_computation.7 | async-start | bytes 7077888 | tf_op jit(solution)/shard_map/reduce_scatter | solution.py:49
  179.6 23.3 %copy-start.6 = (f32[4,128]{1,0:T(4,128)S(1)}, f32[4,128]{1,0:T(4,128)}, u32[]{:S(2)}) copy-start(f32[4,128]{1,0:T(4,128)} %param.12) | copy-start | bytes 6148
  279.1 118.3 %copy-start.2 = (bf16[512,768]{1,0:T(8,128)(2,1)S(1)}, bf16[512,768]{1,0:T(8,128)(2,1)}, u32[]{:S(2)}) copy-start(bf16[512,768]{1,0:T(8,128)(2,1)} %param.9) | copy-start | bytes 2359300
Sparse Core Ops, SparseCore 0:
  9.6 99.5 all-gather.8
  110.7 32.9 all-gather.10
  145.3 34.9 all-gather.16
  181.7 10.1 all-gather.12
  193.4 10.1 all-gather.20
  205.0 17.9 all-gather.14
  224.5 34.9 all-gather.18
  279.3 118.1 reduce-scatter.1
where the time goes:
time: 410 us; the launch traced here: 406 us
  waiting for transfers between devices  272 us (66%)
  matrix products  82.4 us (20%)
  local copies, waits for them, and re-layouts  21.5 us (5%)
  other arithmetic  16.2 us (4%)
  between operations  13.6 us (3%)
    reduce_scatter x1, waiting for transfers between devices, shards(): lax.psum_scatter(branch_terms.astype(jnp.bfloat16), 'mp', scatter_dimensi...  118 us
    all_gather x1, waiting for transfers between devices, shards(): gathered = lax.all_gather(tokens, 'mp', axis=1, tiled=True)  88.4 us
    all_gather x2, waiting for transfers between devices, shards(): pieces = lax.all_gather((out_weight, mlp_out), 'dp', axis=1, tiled=True)  33.9 us
    all_gather x1, waiting for transfers between devices, shards(): lax.all_gather(qkv_local, 'dp', axis=0, tiled=True)  28.2 us
    dot_general x1, matrix products, shards(): pre_act = jnp.dot(normed, pieces[1], preferred_element_type=jnp.float32)  22.4 us
    dot_general x1, matrix products, shards(): jnp.dot(hidden, pieces[1], preferred_element_type=jnp.float32)  19.6 us
    dot_general x1, matrix products, shards(): projected = jnp.dot(normed, pieces[0], preferred_element_type=jnp.float32)  17.6 us
    unnamed x18, local copies, waits for them, and re-layouts  16.9 us
  transfers between devices with their start and end apart: 8, of which 6 were waited for; matrix products, arithmetic and copies ran while one was open for 24% of the time, Pallas kernels for 0%

commit v1 on v0

--- a/solution.py
+++ b/solution.py
@@ -1,8 +1,11 @@
+import functools
 import math
 
 import jax
 import jax.numpy as jnp
 from jax import lax
+from jax.experimental import pallas as pl
+from jax.experimental.pallas import tpu as pltpu
 from jax.sharding import PartitionSpec as P
 
 EPSILON = 1e-06
@@ -52,9 +55,492 @@
     return (tokens.astype(jnp.float32) + summed).astype(jnp.bfloat16)
 
 
+PLANES = 4
+SLOTS = 4
+BF16 = jnp.bfloat16
+F32 = jnp.float32
+
+
+def remote(src, dst, send, recv, device):
+    return pltpu.make_async_remote_copy(
+        src_ref=src, dst_ref=dst, send_sem=send, recv_sem=recv, device_id=device,
+        device_id_type=pl.DeviceIdType.MESH,
+    )
+
+
+def fused(
+    rows_at_once, chunk,
+    tok, gain, wq_hbm, q_gain, k_gain, wo_hbm, wi_hbm, bias, wm_hbm, out,
+    weights, total, shards_in, stage, swap, cat, from_line, from_plane, final, normed, stats, qb, kb, vb,
+    w_sem, s_send, s_recv, g_send, g_recv, d_send, e_send, e_recv, a_send, a_recv, h_send, h_recv,
+    y_send, y_recv, z_send, z_recv, f_send, f_recv,
+):
+    m = lax.axis_index("mp")
+    c = lax.axis_index("dp")
+    y, z = lax.rem(m, 2), m // 2
+    here = z // 2
+    peers = stats.shape[0]
+    local, width = tok.shape
+    size = rows_at_once
+    half_pieces = local // size
+    pieces = 2 * half_pieces
+    depth = wi_hbm.shape[0]
+    head_cols, units = wo_hbm.shape[0], wi_hbm.shape[1]
+    own_cols, own_units = head_cols // 2, units // 2
+    columns = 3 * head_cols + units
+    head_size = q_gain.shape[1]
+    heads = own_cols // head_size
+    inner = head_cols + units
+    side_line = {"mp": z * 2 + 1 - y}
+    side_core = {"dp": 1 - c}
+    below, above = {"mp": m - 2}, {"mp": m + 2}
+    near = jnp.where(c == 0, jnp.where(z == 0, 0, 1), jnp.where(z == PLANES - 1, 1, 0))
+
+    def lane(start, extent):
+        return pl.ds(pl.multiple_of(start, 128), extent)
+
+    def piece(p):
+        return pl.ds(pl.multiple_of(p * size, size), size)
+
+    first_weights = [
+        pltpu.make_async_copy(
+            wq_hbm.at[t], weights.at[pl.ds(0, depth), pl.ds(t * head_cols, head_cols)], w_sem.at[t]
+        )
+        for t in range(3)
+    ] + [
+        pltpu.make_async_copy(
+            wi_hbm, weights.at[pl.ds(0, depth), pl.ds(3 * head_cols, units)], w_sem.at[3]
+        )
+    ]
+    for copy in first_weights:
+        copy.start()
+
+    barrier = pltpu.get_barrier_semaphore()
+    for k in range(1, peers):
+        pl.semaphore_signal(
+            barrier, inc=1, device_id={"mp": lax.rem(m + k, peers)}, device_id_type=pl.DeviceIdType.MESH
+        )
+    pl.semaphore_signal(barrier, inc=1, device_id=side_core, device_id_type=pl.DeviceIdType.MESH)
+
+    values = tok[...].astype(F32)
+    centre = jnp.mean(values, axis=1, keepdims=True)
+    spread = jnp.sum(jnp.square(values - centre), axis=1, keepdims=True)
+    even = lax.broadcasted_iota(jnp.int32, (local, 128), 1) % 2 == 0
+    tile = jnp.where(even, centre, spread)
+    stats[m] = jnp.transpose(tile)[0:8, :]
+
+    pl.semaphore_wait(barrier, peers)
+    for k in range(1, peers):
+        other = lax.rem(m + k, peers)
+        remote(stats.at[m], stats.at[m], s_send.at[k], s_recv.at[m], {"mp": other}).start()
+    total[...] = jnp.zeros_like(total)
+    for k in range(1, peers):
+        other = lax.rem(m + k, peers)
+        remote(stats.at[other], stats.at[other], s_send.at[k], s_recv.at[other], {"mp": other}).wait_recv()
+    means = [stats[k, 0:1, :] for k in range(peers)]
+    mean = functools.reduce(jnp.add, means) * (1.0 / peers)
+    squares = functools.reduce(jnp.add, [stats[k, 1:2, :] for k in range(peers)])
+    squares = squares + width * functools.reduce(jnp.add, [jnp.square(v - mean) for v in means])
+    scale = lax.rsqrt(squares * (1.0 / (width * peers)) + EPSILON)
+    even_row = lax.broadcasted_iota(jnp.int32, (128, local), 0) % 2 == 0
+    tile = jnp.transpose(jnp.where(even_row, mean, scale))
+    values = tok[...].astype(F32)
+    normed[...] = ((values - tile[:, 0:1]) * tile[:, 1:2] * gain[pl.ds(m, 1), :]).astype(BF16)
+
+    own_slot = lax.rem(m, SLOTS)
+
+    @pl.when(c == here)
+    def _():
+        shards_in[own_slot, pl.ds(pl.multiple_of(c * local, local), local), :] = normed[...]
+
+    def to_core(p):
+        target = shards_in.at[own_slot, piece(c * half_pieces + p)]
+        return remote(
+            normed.at[piece(p)], target, d_send.at[p], g_recv.at[own_slot, c * half_pieces + p], side_core
+        )
+
+    @pl.when(c != here)
+    def _():
+        for p in range(half_pieces):
+            to_core(p).start()
+
+    def shard_piece(slot, p):
+        return shards_in.at[slot, piece(p)]
+
+    def gather(slot, p, way, device):
+        ref = shard_piece(slot, p)
+        return remote(ref, ref, g_send.at[slot, p, way], g_recv.at[slot, p], device)
+
+    def multiply(slot, p):
+        part = shards_in[slot, piece(p), :]
+        depth_at = pl.ds(pl.multiple_of(slot * width, width), width)
+
+        def column_step(j, carry):
+            at = lane(j * chunk, chunk)
+            total[piece(p), at] += jnp.dot(part, weights[depth_at, at], preferred_element_type=F32)
+            return carry
+
+        lax.fori_loop(0, columns // chunk, column_step, 0)
+
+    def own_order(t):
+        p = lax.rem(lax.rem(t, pieces) + c * half_pieces, pieces)
+        return jnp.where(t < pieces, near, 1 - near), p
+
+    def own_line(t, carry):
+        zi, p = own_order(t)
+        origin = 2 * c + zi
+        slot = zi * 2 + y
+
+        @pl.when((z != origin) | (p // half_pieces != c))
+        def _():
+            gather(slot, p, 2, side_line).wait_recv()
+
+        @pl.when((z <= origin) & (z > 0))
+        def _():
+            gather(slot, p, 0, below).start()
+
+        @pl.when((z >= origin) & (z < PLANES - 1))
+        def _():
+            gather(slot, p, 1, above).start()
+
+        gather(slot, p, 2, side_line).start()
+
+        @pl.when(t == 0)
+        def _():
+            for copy in first_weights:
+                copy.wait()
+
+        multiply(slot, p)
+        return carry
+
+    lax.fori_loop(0, 2 * pieces, own_line, 0)
+
+    def exchange(part, p):
+        return remote(
+            stage.at[part, piece(p)], swap.at[part, piece(p)], e_send.at[part, p], e_recv.at[part, p], side_core
+        )
+
+    def other_line(t, carry):
+        zi, p = own_order(t)
+        slot = zi * 2 + 1 - y
+        gather(slot, p, 2, side_line).wait_recv()
+        multiply(slot, p)
+
+        @pl.when(t >= pieces)
+        def _():
+            for part in range(3):
+                stage[0, piece(p), pl.ds(part * own_cols, own_cols)] = total[
+                    piece(p), lane(part * head_cols + (1 - c) * own_cols, own_cols)
+                ].astype(BF16)
+            exchange(0, p).start()
+            stage[1, piece(p), pl.ds(0, own_units)] = total[
+                piece(p), lane(3 * head_cols + (1 - c) * own_units, own_units)
+            ].astype(BF16)
+            exchange(1, p).start()
+
+        return carry
+
+    lax.fori_loop(0, 2 * pieces, other_line, 0)
+
+    second_weights = [
+        pltpu.make_async_copy(wo_hbm, weights.at[pl.ds(0, head_cols), pl.ds(0, depth)], w_sem.at[0]),
+        pltpu.make_async_copy(wm_hbm, weights.at[pl.ds(head_cols, units), pl.ds(0, depth)], w_sem.at[1]),
+    ]
+    for copy in second_weights:
+        copy.start()
+
+    def heads_in(t, carry):
+        _, p = own_order(t)
+        exchange(0, p).wait_recv()
+        for part, (target, gains) in enumerate(((qb, q_gain), (kb, k_gain), (vb, None))):
+            for head in range(heads):
+                at = part * own_cols + head * head_size
+                block = total[
+                    piece(p), lane(part * head_cols + c * own_cols + head * head_size, head_size)
+                ] + swap[0, piece(p), pl.ds(at, head_size)].astype(F32)
+                if gains is not None:
+                    block = normalize(block) * gains[pl.ds(c * heads + head, 1), :]
+                target[piece(p), pl.ds(head * head_size, head_size)] = block.astype(BF16)
+        return carry
+
+    lax.fori_loop(0, pieces, heads_in, 0)
+
+    def attended_copy(p):
+        ref = cat.at[piece(p), lane(c * own_cols, own_cols)]
+        return remote(ref, ref, a_send.at[p], a_recv.at[p], side_core)
+
+    def attended_back(p):
+        ref = cat.at[piece(p), lane((1 - c) * own_cols, own_cols)]
+        return remote(ref, ref, a_send.at[p], a_recv.at[p], side_core)
+
+    def hidden_copy(p):
+        ref = cat.at[piece(p), lane(head_cols + c * own_units, own_units)]
+        return remote(ref, ref, h_send.at[p], h_recv.at[p], side_core)
+
+    def hidden_back(p):
+        ref = cat.at[piece(p), lane(head_cols + (1 - c) * own_units, own_units)]
+        return remote(ref, ref, h_send.at[p], h_recv.at[p], side_core)
+
+    def attend(t, carry):
+        _, p = own_order(t)
+        for head in range(heads):
+            at = pl.ds(head * head_size, head_size)
+            scores = lax.dot_general(
+                qb[piece(p), at], kb[:, at], (((1,), (1,)), ((), ())), preferred_element_type=F32
+            )
+            top = jnp.max(scores, axis=1, keepdims=True)
+            powers = jnp.exp((scores - top) * (1.0 / math.sqrt(head_size)))
+            norm = jnp.sum(powers, axis=1, keepdims=True)
+            result = jnp.dot(powers.astype(BF16), vb[:, at], preferred_element_type=F32) / norm
+            cat[piece(p), lane(c * own_cols + head * head_size, head_size)] = result.astype(BF16)
+        attended_copy(p).start()
+        return carry
+
+    lax.fori_loop(0, pieces, attend, 0)
+
+    def activate(t, carry):
+        _, p = own_order(t)
+        exchange(1, p).wait_recv()
+        mine = lane(3 * head_cols + c * own_units, own_units)
+        before = total[piece(p), mine] + swap[1, piece(p), pl.ds(0, own_units)].astype(F32)
+        before = before + bias[:, lane(c * own_units, own_units)]
+        active = 0.5 * before * (1.0 + lax.erf(before * (1.0 / math.sqrt(2.0))))
+        cat[piece(p), lane(head_cols + c * own_units, own_units)] = active.astype(BF16)
+        hidden_copy(p).start()
+        return carry
+
+    lax.fori_loop(0, pieces, activate, 0)
+
+    def sent(t, carry):
+        zi, p = own_order(t)
+        origin = 2 * c + zi
+        slot = zi * 2 + y
+
+        @pl.when((z <= origin) & (z > 0))
+        def _():
+            gather(slot, p, 0, below).wait_send()
+
+        @pl.when((z >= origin) & (z < PLANES - 1))
+        def _():
+            gather(slot, p, 1, above).wait_send()
+
+        gather(slot, p, 2, side_line).wait_send()
+
+        @pl.when(t < pieces)
+        def _():
+            for part in range(2):
+                exchange(part, p).wait_send()
+
+        return carry
+
+    lax.fori_loop(0, 2 * pieces, sent, 0)
+    for k in range(1, peers):
+        remote(stats.at[m], stats.at[m], s_send.at[k], s_recv.at[m], side_line).wait_send()
+
+    @pl.when(c != here)
+    def _():
+        for p in range(half_pieces):
+            to_core(p).wait_send()
+
+    for copy in second_weights:
+        copy.wait()
+
+    def out_order(t):
+        p = lax.rem(lax.rem(t, pieces) + (1 - c) * half_pieces, pieces)
+        return jnp.where(t < pieces, 1 - near, near), p
+
+    def term(p, block):
+        return jnp.dot(
+            cat[piece(p), :], weights[pl.ds(0, inner), lane(block * width, width)], preferred_element_type=F32
+        )
+
+    def to_line(zi, p):
+        return remote(
+            stage.at[zi, piece(p)], from_line.at[zi, piece(p)], y_send.at[zi, p], y_recv.at[zi, p], side_line
+        )
+
+    def other_terms(t, carry):
+        zi, p = out_order(t)
+
+        @pl.when(t < pieces)
+        def _():
+            attended_back(p).wait_recv()
+            hidden_back(p).wait_recv()
+
+        stage[zi, piece(p), :] = term(p, zi * 2 + 1 - y).astype(BF16)
+        to_line(zi, p).start()
+        return carry
+
+    lax.fori_loop(0, 2 * pieces, other_terms, 0)
+
+    def own_terms(t, carry):
+        zi, p = out_order(t)
+        total[piece(p), lane(zi * width, width)] = term(p, zi * 2 + y)
+        return carry
+
+    lax.fori_loop(0, 2 * pieces, own_terms, 0)
+
+    def to_plane(zi, p):
+        up = jnp.where(z < 2 * c + zi, 1, 0)
+        return remote(
+            shards_in.at[zi, piece(p)], from_plane.at[zi, 1 - up, piece(p)],
+            z_send.at[zi, p], z_recv.at[zi, 1 - up, p], {"mp": m + 4 * up - 2},
+        )
+
+    def arrival(zi, side, p):
+        ref = from_plane.at[zi, side, piece(p)]
+        return remote(ref, ref, z_send.at[zi, p], z_recv.at[zi, side, p], side_line)
+
+    def to_owner(zi, p):
+        q = lax.rem(p, half_pieces)
+        return remote(shards_in.at[zi, piece(p)], final.at[piece(q)], f_send.at[q], f_recv.at[q], side_core)
+
+    def reduce_step(t, carry):
+        zi, p = out_order(t)
+        goal = 2 * c + zi
+        at = lane(zi * width, width)
+        to_line(zi, p).wait_recv()
+        total[piece(p), at] += from_line[zi, piece(p), :].astype(F32)
+
+        @pl.when((z <= goal) & (z > 0))
+        def _():
+            arrival(zi, 0, p).wait_recv()
+            total[piece(p), at] += from_plane[zi, 0, piece(p), :].astype(F32)
+
+        @pl.when((z >= goal) & (z < PLANES - 1))
+        def _():
+            arrival(zi, 1, p).wait_recv()
+            total[piece(p), at] += from_plane[zi, 1, piece(p), :].astype(F32)
+
+        @pl.when(z != goal)
+        def _():
+            shards_in[zi, piece(p), :] = total[piece(p), at].astype(BF16)
+            to_plane(zi, p).start()
+
+        @pl.when((z == goal) & (p // half_pieces != c))
+        def _():
+            shards_in[zi, piece(p), :] = total[piece(p), at].astype(BF16)
+            to_owner(zi, p).start()
+
+        @pl.when((z == goal) & (p // half_pieces == c))
+        def _():
+            q = lax.rem(p, half_pieces)
+            out[piece(q), :] = (tok[piece(q), :].astype(F32) + total[piece(p), at]).astype(BF16)
+
+        return carry
+
+    lax.fori_loop(0, 2 * pieces, reduce_step, 0)
+
+    @pl.when(c != here)
+    def _():
+        for q in range(half_pieces):
+            ref = final.at[piece(q)]
+            remote(ref, ref, f_send.at[q], f_recv.at[q], side_core).wait_recv()
+            out[piece(q), :] = (tok[piece(q), :].astype(F32) + final[piece(q), :].astype(F32)).astype(BF16)
+
+    def finish(t, carry):
+        zi, p = out_order(t)
+        to_line(zi, p).wait_send()
+
+        @pl.when(z != 2 * c + zi)
+        def _():
+            to_plane(zi, p).wait_send()
+
+        @pl.when((z == 2 * c + zi) & (p // half_pieces != c))
+        def _():
+            to_owner(zi, p).wait_send()
+
+        @pl.when(t < pieces)
+        def _():
+            attended_copy(p).wait_send()
+            hidden_copy(p).wait_send()
+
+        return carry
+
+    lax.fori_loop(0, 2 * pieces, finish, 0)
+
+
+def fused_shards(tokens, ln_gain, qkv_weight, q_gain, k_gain, out_weight, mlp_in, mlp_bias, mlp_out):
+    local, width = tokens.shape
+    depth, _, head_cols = qkv_weight.shape
+    units = mlp_in.shape[1]
+    half = out_weight.shape[1]
+    peers = ln_gain.shape[0] // width
+    rows = 2 * local
+    size = local // HALF_PIECES
+    pieces = 2 * HALF_PIECES
+    columns = 3 * head_cols + units
+    inner = head_cols + units
+    chunk = 512
+    vmem, hbm = pl.BlockSpec(memory_space=pltpu.VMEM), pl.BlockSpec(memory_space=pl.ANY)
+    dma = pltpu.SemaphoreType.DMA
+    return pl.pallas_call(
+        functools.partial(fused, size, chunk),
+        out_shape=jax.ShapeDtypeStruct(tokens.shape, BF16),
+        in_specs=[vmem, vmem, hbm, vmem, vmem, hbm, hbm, vmem, hbm],
+        out_specs=vmem,
+        scratch_shapes=[
+            pltpu.VMEM((max(depth, inner), max(columns, half)), BF16),
+            pltpu.VMEM((rows, columns), F32),
+            pltpu.VMEM((SLOTS, rows, width), BF16),
+            pltpu.VMEM((2, rows, width), BF16),
+            pltpu.VMEM((2, rows, width), BF16),
+            pltpu.VMEM((rows, inner), BF16),
+            pltpu.VMEM((2, rows, width), BF16),
+            pltpu.VMEM((2, 2, rows, width), BF16),
+            pltpu.VMEM((local, width), BF16),
+            pltpu.VMEM((local, width), BF16),
+            pltpu.VMEM((peers, 8, local), F32),
+            pltpu.VMEM((rows, head_cols // 2), BF16),
+            pltpu.VMEM((rows, head_cols // 2), BF16),
+            pltpu.VMEM((rows, head_cols // 2), BF16),
+            dma((4,)), dma((peers,)), dma((peers,)), dma((SLOTS, pieces, 3)), dma((SLOTS, pieces)),
+            dma((HALF_PIECES,)), dma((2, pieces)), dma((2, pieces)),
+            dma((pieces,)), dma((pieces,)), dma((pieces,)), dma((pieces,)),
+            dma((2, pieces)), dma((2, pieces)), dma((2, pieces)), dma((2, 2, pieces)),
+            dma((HALF_PIECES,)), dma((HALF_PIECES,)),
+        ],
+        compiler_params=pltpu.CompilerParams(
+            collective_id=0, has_side_effects=True, vmem_limit_bytes=VMEM_BYTES
+        ),
+    )(
+        tokens, ln_gain.reshape(peers, width), jnp.transpose(qkv_weight, (1, 0, 2)), q_gain, k_gain,
+        out_weight, mlp_in, mlp_bias.reshape(1, units), mlp_out,
+    )
+
+
+HALF_PIECES = 2
+VMEM_BYTES = 63 * 1024 * 1024
+
+
+def fits(mesh, tokens, ln_gain, qkv_weight, q_gain, k_gain, out_weight, mlp_in, mlp_bias, mlp_out):
+    peers, cores = mesh.shape["mp"], mesh.shape["dp"]
+    if peers != 2 * PLANES or cores != 2:
+        return False
+    local = tokens.shape[0] // (mesh.shape["pool"] * cores)
+    width = tokens.shape[1] // peers
+    head_cols = out_weight.shape[0] // peers
+    units = mlp_in.shape[1] // peers
+    columns = 3 * head_cols + units
+    return (
+        local % (16 * HALF_PIECES) == 0 and local % 128 == 0 and width % 128 == 0
+        and q_gain.shape[1] == 128 and head_cols % 256 == 0 and units % 256 == 0 and columns % 512 == 0
+        and max(3 * head_cols // 2, units // 2) <= width and 2 * width <= columns
+        and local * peers * width <= 512 * 6144 and head_cols <= 512 and units <= 1536
+    )
+
+
 def solution(mesh):
+    def run(*args):
+        body = fused_shards if fits(mesh, *args) else shards
+        return mapped(mesh, body)(*args)
+
+    return run
+
+
+def mapped(mesh, body):
     return jax.shard_map(
-        shards,
+        body,
         mesh=mesh,
         in_specs=(
             P(("pool", "dp"), "mp"),

time: 410 us -> 183 us (0.45)
  waiting for transfers between devices: 272 us -> 0 us
  Pallas kernels: 0 us -> 178 us
  matrix products: 82.4 us -> 0 us
  local copies, waits for them, and re-layouts: 21.5 us -> 4.7 us
  other arithmetic: 16.2 us -> 0 us
  between operations: 13.6 us -> 0.01 us
    pallas_call x0 -> x1, Pallas kernels: none -> 178 us  [fused_shards(): pl.pallas_call(functools.partial(fused, size, chunk), out_shape=jax.Shape...]
    all_gather x7 -> x0, waiting for transfers between devices: 151 us -> none  [the longest x1 88.4 us: shards(): gathered = lax.all_gather(tokens, 'mp', axis=1, tiled=True)]
    reduce_scatter x1 -> x0, waiting for transfers between devices: 118 us -> none  [shards(): lax.psum_scatter(branch_terms.astype(jnp.bfloat16), 'mp', scatter_dimensi...]
    dot_general x5 -> x0, matrix products: 75.1 us -> none  [the longest x1 22.4 us: shards(): pre_act = jnp.dot(normed, pieces[1], preferred_element_type=jnp.float32)]
    unnamed x18 -> x1, local copies, waits for them, and re-layouts: 16.9 us -> 2.06 us
    reduce_sum x5 -> x0, other arithmetic: 11.6 us -> none  [the longest x2 6.95 us: normalize(): centre = jnp.mean(values, axis=-1, keepdims=True)]
    sub x1 -> x0, matrix products: 7.26 us -> none  [shards(): probs = jax.nn.softmax(scores, axis=-1).astype(jnp.bfloat16)]
    convert_element_type x2 -> x0, other arithmetic: 4.64 us -> none  [the longest x1 2.44 us: shards(): key_rows = (normalize(projected[:, 1]) * k_gain).astype(jnp.bfloat16)]
  transfers between devices with their start and end apart: 8 -> 0, of which waited for: 6 -> 0; matrix products, arithmetic and copies ran while one was open for 24% -> 0% of each run, Pallas kernels for 0% -> 0%
where the time goes in v1:
time: 183 us
  Pallas kernels  178 us (97%)
  local copies, waits for them, and re-layouts  4.7 us (3%)
    pallas_call x1, Pallas kernels, fused_shards(): pl.pallas_call(functools.partial(fused, size, chunk), out_shape=jax.Shape...  178 us

profile of v1, /device:TPU:8, one launch (start us, length us, event | category | flops | bytes accessed | tf_op | source)
XLA Modules:
  0.0 182.5 jit_solution(16808465208869538284)
XLA Ops:
  0.0 1.3 reshape.7.bias
  1.3 1.3 reshape.6.gain
  2.6 177.8 %shard_map.91 = bf16[512,768]{1,0:T(8,128)(2,1)} custom-call(bf16[512,768]{1,0:T(8,128)(2,1)} %tok.1, f32[8,768]{1,0:T(8,128)} %reshape.6.gain, bf16[3,3072,512]{2,1,0:T(8,128)(2,1)} %bitcast.1, f32[4,128]{1,0:T(4,128)} %q_gain.1, f32[4,128]{1,0:T(4,128)} %k_gain.1, bf16[512,3072]{1,0:T(8,128)(2,1)} %wo_hbm.1, bf16[3072,1536]{1,0:T(8,128)(2,1)} %wi_hbm.1, ...), custom_call_target="tpu_custom_call" | custom-call | tf_op jit(solution)/shard_map/pallas_call | solution.py:477
  180.4 2.1 %copy.11 = bf16[512,768]{1,0:T(8,128)(2,1)} copy(bf16[512,768]{1,0:T(8,128)(2,1)} %shard_map.91) | data formatting | bytes 1572864

commit v2 on v1

--- a/solution.py
+++ b/solution.py
@@ -71,9 +71,9 @@
 def fused(
     rows_at_once, chunk,
     tok, gain, wq_hbm, q_gain, k_gain, wo_hbm, wi_hbm, bias, wm_hbm, out,
-    weights, total, shards_in, stage, swap, cat, from_line, from_plane, final, normed, stats, qb, kb, vb,
+    weights, total, shards_in, stage, swap, cat, from_line, from_plane, from_chain, normed, stats, qb, kb, vb,
     w_sem, s_send, s_recv, g_send, g_recv, d_send, e_send, e_recv, a_send, a_recv, h_send, h_recv,
-    y_send, y_recv, z_send, z_recv, f_send, f_recv,
+    y_send, y_recv, z_send, z_recv, c_recv, f_send, f_recv,
 ):
     m = lax.axis_index("mp")
     c = lax.axis_index("dp")
@@ -95,6 +95,13 @@
     side_core = {"dp": 1 - c}
     below, above = {"mp": m - 2}, {"mp": m + 2}
     near = jnp.where(c == 0, jnp.where(z == 0, 0, 1), jnp.where(z == PLANES - 1, 1, 0))
+    outer = (PLANES - 1) * c
+
+    def crosses_once(zi, p):
+        return (zi == c) & (p < half_pieces)
+
+    def crosses_here(zi, p):
+        return (zi != c) | (p >= half_pieces) | (z == outer)
 
     def lane(start, extent):
         return pl.ds(pl.multiple_of(start, 128), extent)
@@ -183,8 +190,7 @@
         lax.fori_loop(0, columns // chunk, column_step, 0)
 
     def own_order(t):
-        p = lax.rem(lax.rem(t, pieces) + c * half_pieces, pieces)
-        return jnp.where(t < pieces, near, 1 - near), p
+        return jnp.where(t < pieces, near, 1 - near), lax.rem(t, pieces)
 
     def own_line(t, carry):
         zi, p = own_order(t)
@@ -203,7 +209,9 @@
         def _():
             gather(slot, p, 1, above).start()
 
-        gather(slot, p, 2, side_line).start()
+        @pl.when(crosses_here(zi, p))
+        def _():
+            gather(slot, p, 2, side_line).start()
 
         @pl.when(t == 0)
         def _():
@@ -211,7 +219,25 @@
                 copy.wait()
 
         multiply(slot, p)
+
+        @pl.when(t >= pieces + half_pieces)
+        def _():
+            other = c * 2 + 1 - y
+            q = p - half_pieces
+            gather(other, q, 2, side_line).wait_recv()
+            pass_on(other, q, lambda copy: copy.start())
+            multiply(other, q)
+
         return carry
+
+    def pass_on(slot, p, act):
+        @pl.when((c == 0) & (z < PLANES - 1))
+        def _():
+            act(gather(slot, p, 1, above))
+
+        @pl.when((c == 1) & (z > 0))
+        def _():
+            act(gather(slot, p, 0, below))
 
     lax.fori_loop(0, 2 * pieces, own_line, 0)
 
@@ -223,8 +249,11 @@
     def other_line(t, carry):
         zi, p = own_order(t)
         slot = zi * 2 + 1 - y
-        gather(slot, p, 2, side_line).wait_recv()
-        multiply(slot, p)
+
+        @pl.when(jnp.logical_not(crosses_once(zi, p)))
+        def _():
+            gather(slot, p, 2, side_line).wait_recv()
+            multiply(slot, p)
 
         @pl.when(t >= pieces)
         def _():
@@ -238,19 +267,13 @@
             ].astype(BF16)
             exchange(1, p).start()
 
+        @pl.when(t > pieces)
+        def _():
+            finish_rows(p - 1)
+
         return carry
 
-    lax.fori_loop(0, 2 * pieces, other_line, 0)
-
-    second_weights = [
-        pltpu.make_async_copy(wo_hbm, weights.at[pl.ds(0, head_cols), pl.ds(0, depth)], w_sem.at[0]),
-        pltpu.make_async_copy(wm_hbm, weights.at[pl.ds(head_cols, units), pl.ds(0, depth)], w_sem.at[1]),
-    ]
-    for copy in second_weights:
-        copy.start()
-
-    def heads_in(t, carry):
-        _, p = own_order(t)
+    def heads_in(p):
         exchange(0, p).wait_recv()
         for part, (target, gains) in enumerate(((qb, q_gain), (kb, k_gain), (vb, None))):
             for head in range(heads):
@@ -261,9 +284,6 @@
                 if gains is not None:
                     block = normalize(block) * gains[pl.ds(c * heads + head, 1), :]
                 target[piece(p), pl.ds(head * head_size, head_size)] = block.astype(BF16)
-        return carry
-
-    lax.fori_loop(0, pieces, heads_in, 0)
 
     def attended_copy(p):
         ref = cat.at[piece(p), lane(c * own_cols, own_cols)]
@@ -281,8 +301,7 @@
         ref = cat.at[piece(p), lane(head_cols + (1 - c) * own_units, own_units)]
         return remote(ref, ref, h_send.at[p], h_recv.at[p], side_core)
 
-    def attend(t, carry):
-        _, p = own_order(t)
+    def attend(p):
         for head in range(heads):
             at = pl.ds(head * head_size, head_size)
             scores = lax.dot_general(
@@ -294,12 +313,8 @@
             result = jnp.dot(powers.astype(BF16), vb[:, at], preferred_element_type=F32) / norm
             cat[piece(p), lane(c * own_cols + head * head_size, head_size)] = result.astype(BF16)
         attended_copy(p).start()
-        return carry
-
-    lax.fori_loop(0, pieces, attend, 0)
-
-    def activate(t, carry):
-        _, p = own_order(t)
+
+    def activate(p):
         exchange(1, p).wait_recv()
         mine = lane(3 * head_cols + c * own_units, own_units)
         before = total[piece(p), mine] + swap[1, piece(p), pl.ds(0, own_units)].astype(F32)
@@ -307,9 +322,21 @@
         active = 0.5 * before * (1.0 + lax.erf(before * (1.0 / math.sqrt(2.0))))
         cat[piece(p), lane(head_cols + c * own_units, own_units)] = active.astype(BF16)
         hidden_copy(p).start()
-        return carry
-
-    lax.fori_loop(0, pieces, activate, 0)
+
+    def finish_rows(p):
+        heads_in(p)
+        activate(p)
+
+    lax.fori_loop(0, 2 * pieces, other_line, 0)
+
+    second_weights = [
+        pltpu.make_async_copy(wo_hbm, weights.at[pl.ds(0, head_cols), pl.ds(0, depth)], w_sem.at[0]),
+        pltpu.make_async_copy(wm_hbm, weights.at[pl.ds(head_cols, units), pl.ds(0, depth)], w_sem.at[1]),
+    ]
+    for copy in second_weights:
+        copy.start()
+
+    finish_rows(pieces - 1)
 
     def sent(t, carry):
         zi, p = own_order(t)
@@ -324,7 +351,13 @@
         def _():
             gather(slot, p, 1, above).wait_send()
 
-        gather(slot, p, 2, side_line).wait_send()
+        @pl.when(crosses_here(zi, p))
+        def _():
+            gather(slot, p, 2, side_line).wait_send()
+
+        @pl.when(t < half_pieces)
+        def _():
+            pass_on(c * 2 + 1 - y, p, lambda copy: copy.wait_send())
 
         @pl.when(t < pieces)
         def _():
@@ -346,7 +379,7 @@
         copy.wait()
 
     def out_order(t):
-        p = lax.rem(lax.rem(t, pieces) + (1 - c) * half_pieces, pieces)
+        p = lax.rem(lax.rem(t, pieces) + half_pieces, pieces)
         return jnp.where(t < pieces, 1 - near, near), p
 
     def term(p, block):
@@ -359,7 +392,7 @@
             stage.at[zi, piece(p)], from_line.at[zi, piece(p)], y_send.at[zi, p], y_recv.at[zi, p], side_line
         )
 
-    def other_terms(t, carry):
+    def other_terms(t):
         zi, p = out_order(t)
 
         @pl.when(t < pieces)
@@ -367,11 +400,48 @@
             attended_back(p).wait_recv()
             hidden_back(p).wait_recv()
 
-        stage[zi, piece(p), :] = term(p, zi * 2 + 1 - y).astype(BF16)
-        to_line(zi, p).start()
+        value = term(p, zi * 2 + 1 - y)
+
+        @pl.when(jnp.logical_not(crosses_once(zi, p)))
+        def _():
+            stage[zi, piece(p), :] = value.astype(BF16)
+            to_line(zi, p).start()
+
+        @pl.when(crosses_once(zi, p) & (z == PLANES - 1 - outer))
+        def _():
+            stage[zi, piece(p), :] = value.astype(BF16)
+
+        @pl.when(crosses_once(zi, p) & (z != PLANES - 1 - outer))
+        def _():
+            q = lax.rem(p, half_pieces)
+            along(zi, q).wait_recv()
+            stage[zi, piece(p), :] = (value + from_chain[piece(q), :].astype(F32)).astype(BF16)
+
+        @pl.when(crosses_once(zi, p) & (z == outer))
+        def _():
+            to_line(zi, p).start()
+
+        @pl.when(crosses_once(zi, p) & (z != outer))
+        def _():
+            along(zi, lax.rem(p, half_pieces)).start()
+
+    def along(zi, q):
+        return remote(
+            stage.at[zi, piece(q)], from_chain.at[piece(q)], y_send.at[zi, q], c_recv.at[q], {"mp": m + 4 * c - 2}
+        )
+
+    def attend_and_terms(t, carry):
+        @pl.when(t < pieces)
+        def _():
+            attend(out_order(t)[1])
+
+        @pl.when(t > 0)
+        def _():
+            other_terms(t - 1)
+
         return carry
 
-    lax.fori_loop(0, 2 * pieces, other_terms, 0)
+    lax.fori_loop(0, 2 * pieces + 1, attend_and_terms, 0)
 
     def own_terms(t, carry):
         zi, p = out_order(t)
@@ -393,14 +463,17 @@
 
     def to_owner(zi, p):
         q = lax.rem(p, half_pieces)
-        return remote(shards_in.at[zi, piece(p)], final.at[piece(q)], f_send.at[q], f_recv.at[q], side_core)
+        return remote(shards_in.at[zi, piece(p)], normed.at[piece(q)], f_send.at[q], f_recv.at[q], side_core)
 
     def reduce_step(t, carry):
         zi, p = out_order(t)
         goal = 2 * c + zi
         at = lane(zi * width, width)
-        to_line(zi, p).wait_recv()
-        total[piece(p), at] += from_line[zi, piece(p), :].astype(F32)
+
+        @pl.when(crosses_here(zi, p))
+        def _():
+            to_line(zi, p).wait_recv()
+            total[piece(p), at] += from_line[zi, piece(p), :].astype(F32)
 
         @pl.when((z <= goal) & (z > 0))
         def _():
@@ -434,9 +507,9 @@
     @pl.when(c != here)
     def _():
         for q in range(half_pieces):
-            ref = final.at[piece(q)]
+            ref = normed.at[piece(q)]
             remote(ref, ref, f_send.at[q], f_recv.at[q], side_core).wait_recv()
-            out[piece(q), :] = (tok[piece(q), :].astype(F32) + final[piece(q), :].astype(F32)).astype(BF16)
+            out[piece(q), :] = (tok[piece(q), :].astype(F32) + normed[piece(q), :].astype(F32)).astype(BF16)
 
     def finish(t, carry):
         zi, p = out_order(t)
@@ -497,7 +570,7 @@
             dma((4,)), dma((peers,)), dma((peers,)), dma((SLOTS, pieces, 3)), dma((SLOTS, pieces)),
             dma((HALF_PIECES,)), dma((2, pieces)), dma((2, pieces)),
             dma((pieces,)), dma((pieces,)), dma((pieces,)), dma((pieces,)),
-            dma((2, pieces)), dma((2, pieces)), dma((2, pieces)), dma((2, 2, pieces)),
+            dma((2, pieces)), dma((2, pieces)), dma((2, pieces)), dma((2, 2, pieces)), dma((HALF_PIECES,)),
             dma((HALF_PIECES,)), dma((HALF_PIECES,)),
         ],
         compiler_params=pltpu.CompilerParams(

time: 183 us -> 186 us (1.016)
  Pallas kernels: 178 us -> 181 us
    pallas_call x1, Pallas kernels: 178 us -> 181 us  [fused_shards(): pl.pallas_call(functools.partial(fused, size, chunk), out_shape=jax.Shape...]
where the time goes in v2:
time: 186 us
  Pallas kernels  181 us (97%)
  local copies, waits for them, and re-layouts  4.7 us (3%)
    pallas_call x1, Pallas kernels, fused_shards(): pl.pallas_call(functools.partial(fused, size, chunk), out_shape=jax.Shape...  181 us

profile of v2, /device:TPU:8, one launch (start us, length us, event | category | flops | bytes accessed | tf_op | source)
XLA Modules:
  0.0 185.7 jit_solution(3710733893761304040)
XLA Ops:
  0.0 1.3 reshape.7.bias
  1.3 1.3 reshape.6.gain
  2.6 181.0 %shard_map.91 = bf16[512,768]{1,0:T(8,128)(2,1)} custom-call(bf16[512,768]{1,0:T(8,128)(2,1)} %tok.1, f32[8,768]{1,0:T(8,128)} %reshape.6.gain, bf16[3,3072,512]{2,1,0:T(8,128)(2,1)} %bitcast.1, f32[4,128]{1,0:T(4,128)} %q_gain.1, f32[4,128]{1,0:T(4,128)} %k_gain.1, bf16[512,3072]{1,0:T(8,128)(2,1)} %wo_hbm.1, bf16[3072,1536]{1,0:T(8,128)(2,1)} %wi_hbm.1, ...), custom_call_target="tpu_custom_call" | custom-call | tf_op jit(solution)/shard_map/pallas_call | solution.py:550
  183.7 2.1 %copy.11 = bf16[512,768]{1,0:T(8,128)(2,1)} copy(bf16[512,768]{1,0:T(8,128)(2,1)} %shard_map.91) | data formatting | bytes 1572864
